TPU v7x, 32 devices: a whole 2x2x4 slice. The times are simulated.
32 devices in a mesh: grp: 2 (over y), band: 16 (over z, x, core).
Axes of the slice: x: 2, y: 2, z: 4, core: 2. Of those that a mesh axis runs over, the one named last changes fastest.
Arguments:
- spec_in: bfloat16 [2, 64, 4656], P(None, 'grp', 'band'), parts along dimension 1, may hold values from -0.625 to 0.625
- forcing: bfloat16 [80, 2, 64, 5248], P('band', None, 'grp'), parts along dimension 2, may hold values from -6 to 6
- legendre: bfloat16 [4656, 80], P('band'), may hold values from -0.625 to 0.625
- weights: float32 [80], replicated, may hold values from 0.003 to 0.03
- cycle_slots: int32 [80], P('band'), may hold values from 0 to 79, each once
- wave_pairs: int32 [48], P('band'), may hold values from 0 to 47, each once
Outputs:
- grid_field: bfloat16 [80, 2, 64, 5248], P('band', None, 'grp'), parts along dimension 2
- spec_out: float32 [2, 64, 4656], P(None, 'grp', 'band'), parts along dimension 1
There are 2 independent parts, one for each index of `grp`. A program takes and returns all parts, laid end to end along the dimension named above; an argument that names none is the same for every part. Nothing has to cross between parts.
Inputs may be any that keep to these rules, and one draw needn't show every extreme that they name: `cycle_slots`: each latitude once. `wave_pairs`: each pair once.
All inputs are finite; a program needn't handle non-finite values.
Results may differ from a plain program's by a relative error of at most 0.0072.
Values may be sent and summed in bfloat16 or wider, within the bound.
A program may use at most 128 MiB of HBM per device.

v0:
```python
import math

import jax
import jax.numpy as jnp
from jax import lax
from jax.sharding import PartitionSpec as P

TRUNC = 1279
NLON_EQ = 5136


two_pi = 2.0 * math.pi


def wave_list(pair_ids, window):
    first_wave = TRUNC + 1 - window + pair_ids
    second_wave = TRUNC - pair_ids
    return jnp.stack([first_wave, second_wave], axis=1).reshape(-1)


def fourier_table(length, wave_numbers, points):
    blocks = points // 128
    high = jnp.arange(blocks, dtype=jnp.int32) * 128
    low = jnp.arange(128, dtype=jnp.int32)
    scale = two_pi / length.astype(jnp.float32)
    angle_high = (wave_numbers[:, None] * high[None, :] % length).astype(jnp.float32) * scale
    angle_low = (wave_numbers[:, None] * low[None, :] % length).astype(jnp.float32) * scale
    cos_high = jnp.cos(angle_high)[:, :, None]
    sin_high = jnp.sin(angle_high)[:, :, None]
    cos_low = jnp.cos(angle_low)[:, None, :]
    sin_low = jnp.sin(angle_low)[:, None, :]
    count = wave_numbers.shape[0]
    cosine = (cos_high * cos_low - sin_high * sin_low).reshape(count, points)
    minus_sine = (-(sin_high * cos_low + cos_high * sin_low)).reshape(count, points)
    inside = (jnp.arange(points, dtype=jnp.int32) < length)[None, :]
    cosine = jnp.where(inside, cosine, jnp.float32(0.0))
    minus_sine = jnp.where(inside, minus_sine, jnp.float32(0.0))
    return jnp.concatenate([cosine, minus_sine], axis=0).astype(jnp.bfloat16)


def row_halves(array, axis):
    widths = [(0, 0)] * array.ndim
    widths[axis] = (0, 1)
    padded = jnp.pad(array, widths)
    shape = list(padded.shape)
    shape[axis : axis + 1] = [shape[axis] // 2, 2]
    folded = padded.reshape(shape)
    even_rows = lax.index_in_dim(folded, 0, axis + 1, keepdims=False)
    odd_rows = lax.index_in_dim(folded, 1, axis + 1, keepdims=False)
    return (even_rows, odd_rows)


def invert_rows(coefficient, legendre_rows, member, flip_sign, form):
    coef_even, coef_odd = row_halves(coefficient, 3)
    leg_even, leg_odd = row_halves(legendre_rows, 1)
    member_even, member_odd = row_halves(member, 1)
    stack_even = jnp.stack(
        [
            coef_even * (1.0 - member_even)[None, None].astype(jnp.bfloat16),
            coef_even * member_even[None, None].astype(jnp.bfloat16),
        ]
    )
    stack_odd = jnp.stack(
        [
            coef_odd * (1.0 - member_odd)[None, None].astype(jnp.bfloat16),
            coef_odd * member_odd[None, None].astype(jnp.bfloat16),
        ]
    )
    sum_even = jnp.einsum(form, stack_even, leg_even, preferred_element_type=jnp.float32)
    sum_odd = jnp.einsum(form, stack_odd, leg_odd, preferred_element_type=jnp.float32)
    north = sum_even + sum_odd
    south = (sum_even - sum_odd) * flip_sign[None, :, None, None, :]
    both = jnp.stack([north, south], axis=1)
    return jnp.transpose(both, (0, 1, 3, 4, 5, 2))


def direct_rows(combined, legendre_rows, member, flip_odd, form):
    leg_even, leg_odd = row_halves(legendre_rows, 1)
    member_even, member_odd = row_halves(member, 1)
    results = []
    for half, leg_half, member_half in ((0, leg_even, member_even), (1, leg_odd, member_odd)):
        first_part = combined[half, :, :, :, :, 0]
        second_part = jnp.where(
            flip_odd[None, None, None, :],
            combined[1 - half, :, :, :, :, 1],
            combined[half, :, :, :, :, 1],
        )
        stacked = jnp.stack([first_part, second_part])
        values = jnp.einsum(form, stacked, leg_half, preferred_element_type=jnp.float32)
        results.append(jnp.where(member_half[None, None] > 0.5, values[1], values[0]))
    merged = jnp.stack(results, axis=-1)
    shape = merged.shape
    merged = merged.reshape(shape[0], shape[1], shape[2], shape[3] * 2)
    return merged[:, :, :, : legendre_rows.shape[1]]


def on_device(spec_in, forcing, legendre, weights, cycle_slots, wave_pairs):
    all_cycles, all_pairs = (
        lax.all_gather(cycle_slots, "band", axis=0, tiled=True),
        lax.all_gather(wave_pairs, "band", axis=0, tiled=True),
    )
    devices = lax.axis_size("band")
    slot_local = wave_pairs.shape[0]
    window = 2 * slot_local * devices
    row_count = window + 1
    level_count = spec_in.shape[1]
    lat_local = cycle_slots.shape[0]
    lat_count = all_cycles.shape[0]
    points = forcing.shape[3]
    offsets = jnp.arange(row_count, dtype=jnp.int32)[None, :]
    boundary = window - wave_pairs
    member = (offsets >= boundary[:, None]).astype(jnp.float32)
    flip_odd = boundary % 2 == 1
    flip_sign = jnp.stack(
        [jnp.ones((slot_local,), jnp.float32), jnp.where(flip_odd, -1.0, 1.0).astype(jnp.float32)]
    )
    coefficient = spec_in.reshape(2, level_count, slot_local, row_count)
    legendre_local = legendre.reshape(slot_local, row_count, lat_count)
    legendre_order = jnp.take(legendre_local, all_cycles, axis=2)
    fourier = invert_rows(
        coefficient, legendre_order, member, flip_sign, "welsr,srq->qwles"
    ).astype(jnp.bfloat16)
    received = lax.all_to_all(fourier, "band", split_axis=0, concat_axis=4, tiled=True)
    received = received.reshape(lat_local, 2 * level_count, 2 * window)
    wave_numbers = wave_list(all_pairs, window)
    lengths = NLON_EQ - 4 * cycle_slots
    force_rows = forcing.reshape(lat_local, 2 * level_count, points)

    def cycle_step(packed):
        fourier_cycle, force_cycle, length = packed
        dft_table = fourier_table(length, wave_numbers, points)
        field_rows = 2.0 * jnp.dot(fourier_cycle, dft_table, preferred_element_type=jnp.float32)
        product = (field_rows * force_cycle.astype(jnp.float32)).astype(jnp.bfloat16)
        returned = lax.dot_general(
            product, dft_table, (((1,), (1,)), ((), ())), preferred_element_type=jnp.float32
        )
        return (field_rows.astype(jnp.bfloat16), returned.astype(jnp.bfloat16))

    fields, returned = lax.map(cycle_step, (received, force_rows, lengths))
    grid_field = fields.reshape(lat_local, 2, level_count, points)
    returned = returned.reshape(lat_local, 2, level_count, 2, window // 2, 2)
    gathered = lax.all_to_all(returned, "band", split_axis=4, concat_axis=0, tiled=True).astype(
        jnp.float32
    )
    north_part = gathered[:, 0]
    south_part = gathered[:, 1]
    lat_weight = jnp.take(weights, all_cycles)[:, None, None, None, None]
    combined = jnp.stack(
        [lat_weight * (north_part + south_part), lat_weight * (north_part - south_part)]
    ).astype(jnp.bfloat16)
    spectral = direct_rows(combined, legendre_order, member, flip_odd, "wqles,srq->wlesr")
    spec_out = jnp.transpose(spectral, (1, 0, 2, 3)).reshape(2, level_count, slot_local * row_count)
    return (grid_field, spec_out)


def solution(mesh):
    in_specs = (
        P(None, "grp", "band"),
        P("band", None, "grp", None),
        P("band", None),
        P(),
        P("band"),
        P("band"),
    )
    out_specs = (P("band", None, "grp", None), P(None, "grp", "band"))
    return jax.shard_map(
        on_device, mesh=mesh, in_specs=in_specs, out_specs=out_specs, check_vma=False
    )
```

profile of v0, /device:TPU:0, one launch (start us, length us, event | category | flops | bytes accessed | tf_op | source)
XLA Modules:
  0.0 107.4 jit_solution(3683719970430602174)
XLA Ops:
  2.0 1.2 %dynamic-slice = u32[1]{0:T(128)} dynamic-slice(u32[32]{0:T(128)} %constant.118, u32[]{:T(128)S(6)} %add.92), dynamic_slice_sizes={1} | dynamic-slice | bytes 12
  6.3 13.7 %all-reduce.6 = (s32[80]{0:T(128)S(1)}, s32[48]{0:T(128)S(1)}) all-reduce(s32[80]{0:T(128)S(1)} %dynamic-update-slice, s32[48]{0:T(128)S(1)} %dynamic-update-slice.1), channel_id=1, replica_groups=mesh['grp'=2,'band'=16] {'band'}, use_global_device_ids=true, to_apply=%add.4 | all-reduce | flops 128 | bytes 1024
  20.1 1.2 %gather_fusion.1 = f32[80]{0:T(128)S(1)} fusion(f32[80]{0:T(128)S(1)} %copy-done, s32[1024]{0:T(1024)S(1)} %pad_clamp_fusion), kind=kCustom, calls=%fused_computation.1 | custom fusion | bytes 960 | tf_op jit(solution)/shard_map/jit(_take)/gather | solution.py:147
  27.6 3.5 %all-to-all-start = ((bf16[16,2,1920]{2,1,0:T(2,128)(2,1)}), bf16[16,2,1920]{2,1,0:T(2,128)(2,1)S(1)}, u32[]{:S(2)}, u32[]{:S(2)}) async-start(bf16[16,2,1920]{2,1,0:T(2,128)(2,1)} %reshape.463), calls=%async_computation | async-start | bytes 245760 | tf_op jit(solution)/shard_map/all_to_all | solution.py:123
  31.4 7.5 %all-to-all-done = bf16[16,2,1920]{2,1,0:T(2,128)(2,1)S(1)} async-done(((bf16[16,2,1920]{2,1,0:T(2,128)(2,1)}), bf16[16,2,1920]{2,1,0:T(2,128)(2,1)S(1)}, u32[]{:S(2)}, u32[]{:S(2)}) %all-to-all-start) | async-done | bytes 122912 | tf_op jit(solution)/shard_map/all_to_all | solution.py:123
  39.9 50.0 %while.13 = (s32[]{:T(128)}, bf16[5,64,5248]{2,1,0:T(8,128)(2,1)}, bf16[5,64,192]{2,1,0:T(8,128)(2,1)S(1)}, bf16[5,64,192]{2,1,0:T(8,128)(2,1)S(1)}, s32[5]{0:T(...) while((s32[]{:T(128)}, bf16[5,64,5248]{2,1,0:T(8,128)(2,1)}, ...), condition=%wide.wide.region_1.2_spmd, body=%wide.wide.region_0.1_spmd.sunk | while | flops 273411712 | bytes 14445586 | solution.py:139
  44.6 1.5 %multiply_subtract_fusion.4 = (bf16[96,41,128]{2,1,0:T(8,128)(2,1)S(1)}, bf16[96,41,128]{2,1,0:T(8,128)(2,1)S(1)}) fusion(f32[96,128]{1,0:T(8,128)S(1)} %get-tuple-element.228, f32[96,41]{1,0:T(8,128)S(1)} %get-tuple-element.229, f32[96,128]{1,0:T(8,128)S(1)} %get-tuple-element.230, f32[96,41]{1,0:T(8,128)S(1)} %get-tuple-element.231), kind=kLoop, calls=%fused_computation.4.clone.clone.1 | loop fusion | flops 4534272 | bytes 2145024 | tf_op jit(solution)/shard_map/while/body/eval_jaxpr/sub | solution.py:33
  46.7 1.4 %bitcast_dynamic-update-slice_fusion.3 = (bf16[5,64,5248]{2,1,0:T(8,128)(2,1)}, f32[64,5248]{1,0:T(8,128)S(1)}) fusion(bf16[5,64,5248]{2,1,0:T(8,128)(2,1)} %get-tuple-element.250, s32[]{:T(128)S(6)} %copy.161, bf16[96,5248]{1,0:T(8,128)(2,1)S(1)} %get-tuple-element.234, bf16[96,5248]{1,0:T(8,128)(2,1)S(1)} %get-tuple-element.235, ...), kind=kOutput, calls=%fused_computation.17.clone.clone.1 | convolution fusion | flops 133677056 | bytes 4064256 | tf_op jit(solution)/shard_map/while/body/eval_jaxpr/dot_general | solution.py:132
  48.0 1.8 %fusion.82 = bf16[5,64,192]{2,1,0:T(8,128)(2,1)S(1)} fusion(bf16[5,64,192]{2,1,0:T(8,128)(2,1)S(1)} %get-tuple-element.251, s32[]{:T(128)S(6)} %copy.161, bf16[96,5248]{1,0:T(8,128)(2,1)S(1)} %get-tuple-element.234, bf16[96,5248]{1,0:T(8,128)(2,1)S(1)} %get-tuple-element.235, f32[64,5248]{1,0:T(8,128)S(1)} %get-tuple-element.237, ...), kind=kOutput, calls=%fused_computation.15.clone.clone.1 | convolution fusion | flops 134025216 | bytes 4064256 | tf_op jit(solution)/shard_map/while/body/eval_jaxpr/dot_general | solution.py:134
  54.6 1.5 %multiply_subtract_fusion.4 = (bf16[96,41,128]{2,1,0:T(8,128)(2,1)S(1)}, bf16[96,41,128]{2,1,0:T(8,128)(2,1)S(1)}) fusion(f32[96,128]{1,0:T(8,128)S(1)} %get-tuple-element.228, f32[96,41]{1,0:T(8,128)S(1)} %get-tuple-element.229, f32[96,128]{1,0:T(8,128)S(1)} %get-tuple-element.230, f32[96,41]{1,0:T(8,128)S(1)} %get-tuple-element.231), kind=kLoop, calls=%fused_computation.4.clone.clone.1 | loop fusion | flops 4534272 | bytes 2145024 | tf_op jit(solution)/shard_map/while/body/eval_jaxpr/sub | solution.py:33
  56.7 1.4 %bitcast_dynamic-update-slice_fusion.3 = (bf16[5,64,5248]{2,1,0:T(8,128)(2,1)}, f32[64,5248]{1,0:T(8,128)S(1)}) fusion(bf16[5,64,5248]{2,1,0:T(8,128)(2,1)} %get-tuple-element.250, s32[]{:T(128)S(6)} %copy.161, bf16[96,5248]{1,0:T(8,128)(2,1)S(1)} %get-tuple-element.234, bf16[96,5248]{1,0:T(8,128)(2,1)S(1)} %get-tuple-element.235, ...), kind=kOutput, calls=%fused_computation.17.clone.clone.1 | convolution fusion | flops 133677056 | bytes 4064256 | tf_op jit(solution)/shard_map/while/body/eval_jaxpr/dot_general | solution.py:132
  58.1 1.8 %fusion.82 = bf16[5,64,192]{2,1,0:T(8,128)(2,1)S(1)} fusion(bf16[5,64,192]{2,1,0:T(8,128)(2,1)S(1)} %get-tuple-element.251, s32[]{:T(128)S(6)} %copy.161, bf16[96,5248]{1,0:T(8,128)(2,1)S(1)} %get-tuple-element.234, bf16[96,5248]{1,0:T(8,128)(2,1)S(1)} %get-tuple-element.235, f32[64,5248]{1,0:T(8,128)S(1)} %get-tuple-element.237, ...), kind=kOutput, calls=%fused_computation.15.clone.clone.1 | convolution fusion | flops 134025216 | bytes 4064256 | tf_op jit(solution)/shard_map/while/body/eval_jaxpr/dot_general | solution.py:134
  64.6 1.5 %multiply_subtract_fusion.4 = (bf16[96,41,128]{2,1,0:T(8,128)(2,1)S(1)}, bf16[96,41,128]{2,1,0:T(8,128)(2,1)S(1)}) fusion(f32[96,128]{1,0:T(8,128)S(1)} %get-tuple-element.228, f32[96,41]{1,0:T(8,128)S(1)} %get-tuple-element.229, f32[96,128]{1,0:T(8,128)S(1)} %get-tuple-element.230, f32[96,41]{1,0:T(8,128)S(1)} %get-tuple-element.231), kind=kLoop, calls=%fused_computation.4.clone.clone.1 | loop fusion | flops 4534272 | bytes 2145024 | tf_op jit(solution)/shard_map/while/body/eval_jaxpr/sub | solution.py:33
  66.7 1.4 %bitcast_dynamic-update-slice_fusion.3 = (bf16[5,64,5248]{2,1,0:T(8,128)(2,1)}, f32[64,5248]{1,0:T(8,128)S(1)}) fusion(bf16[5,64,5248]{2,1,0:T(8,128)(2,1)} %get-tuple-element.250, s32[]{:T(128)S(6)} %copy.161, bf16[96,5248]{1,0:T(8,128)(2,1)S(1)} %get-tuple-element.234, bf16[96,5248]{1,0:T(8,128)(2,1)S(1)} %get-tuple-element.235, ...), kind=kOutput, calls=%fused_computation.17.clone.clone.1 | convolution fusion | flops 133677056 | bytes 4064256 | tf_op jit(solution)/shard_map/while/body/eval_jaxpr/dot_general | solution.py:132
  68.1 1.8 %fusion.82 = bf16[5,64,192]{2,1,0:T(8,128)(2,1)S(1)} fusion(bf16[5,64,192]{2,1,0:T(8,128)(2,1)S(1)} %get-tuple-element.251, s32[]{:T(128)S(6)} %copy.161, bf16[96,5248]{1,0:T(8,128)(2,1)S(1)} %get-tuple-element.234, bf16[96,5248]{1,0:T(8,128)(2,1)S(1)} %get-tuple-element.235, f32[64,5248]{1,0:T(8,128)S(1)} %get-tuple-element.237, ...), kind=kOutput, calls=%fused_computation.15.clone.clone.1 | convolution fusion | flops 134025216 | bytes 4064256 | tf_op jit(solution)/shard_map/while/body/eval_jaxpr/dot_general | solution.py:134
  74.7 1.5 %multiply_subtract_fusion.4 = (bf16[96,41,128]{2,1,0:T(8,128)(2,1)S(1)}, bf16[96,41,128]{2,1,0:T(8,128)(2,1)S(1)}) fusion(f32[96,128]{1,0:T(8,128)S(1)} %get-tuple-element.228, f32[96,41]{1,0:T(8,128)S(1)} %get-tuple-element.229, f32[96,128]{1,0:T(8,128)S(1)} %get-tuple-element.230, f32[96,41]{1,0:T(8,128)S(1)} %get-tuple-element.231), kind=kLoop, calls=%fused_computation.4.clone.clone.1 | loop fusion | flops 4534272 | bytes 2145024 | tf_op jit(solution)/shard_map/while/body/eval_jaxpr/sub | solution.py:33
  76.7 1.4 %bitcast_dynamic-update-slice_fusion.3 = (bf16[5,64,5248]{2,1,0:T(8,128)(2,1)}, f32[64,5248]{1,0:T(8,128)S(1)}) fusion(bf16[5,64,5248]{2,1,0:T(8,128)(2,1)} %get-tuple-element.250, s32[]{:T(128)S(6)} %copy.161, bf16[96,5248]{1,0:T(8,128)(2,1)S(1)} %get-tuple-element.234, bf16[96,5248]{1,0:T(8,128)(2,1)S(1)} %get-tuple-element.235, ...), kind=kOutput, calls=%fused_computation.17.clone.clone.1 | convolution fusion | flops 133677056 | bytes 4064256 | tf_op jit(solution)/shard_map/while/body/eval_jaxpr/dot_general | solution.py:132
  78.1 1.8 %fusion.82 = bf16[5,64,192]{2,1,0:T(8,128)(2,1)S(1)} fusion(bf16[5,64,192]{2,1,0:T(8,128)(2,1)S(1)} %get-tuple-element.251, s32[]{:T(128)S(6)} %copy.161, bf16[96,5248]{1,0:T(8,128)(2,1)S(1)} %get-tuple-element.234, bf16[96,5248]{1,0:T(8,128)(2,1)S(1)} %get-tuple-element.235, f32[64,5248]{1,0:T(8,128)S(1)} %get-tuple-element.237, ...), kind=kOutput, calls=%fused_computation.15.clone.clone.1 | convolution fusion | flops 134025216 | bytes 4064256 | tf_op jit(solution)/shard_map/while/body/eval_jaxpr/dot_general | solution.py:134
  84.7 1.5 %multiply_subtract_fusion.4 = (bf16[96,41,128]{2,1,0:T(8,128)(2,1)S(1)}, bf16[96,41,128]{2,1,0:T(8,128)(2,1)S(1)}) fusion(f32[96,128]{1,0:T(8,128)S(1)} %get-tuple-element.228, f32[96,41]{1,0:T(8,128)S(1)} %get-tuple-element.229, f32[96,128]{1,0:T(8,128)S(1)} %get-tuple-element.230, f32[96,41]{1,0:T(8,128)S(1)} %get-tuple-element.231), kind=kLoop, calls=%fused_computation.4.clone.clone.1 | loop fusion | flops 4534272 | bytes 2145024 | tf_op jit(solution)/shard_map/while/body/eval_jaxpr/sub | solution.py:33
  86.7 1.4 %bitcast_dynamic-update-slice_fusion.3 = (bf16[5,64,5248]{2,1,0:T(8,128)(2,1)}, f32[64,5248]{1,0:T(8,128)S(1)}) fusion(bf16[5,64,5248]{2,1,0:T(8,128)(2,1)} %get-tuple-element.250, s32[]{:T(128)S(6)} %copy.161, bf16[96,5248]{1,0:T(8,128)(2,1)S(1)} %get-tuple-element.234, bf16[96,5248]{1,0:T(8,128)(2,1)S(1)} %get-tuple-element.235, ...), kind=kOutput, calls=%fused_computation.17.clone.clone.1 | convolution fusion | flops 133677056 | bytes 4064256 | tf_op jit(solution)/shard_map/while/body/eval_jaxpr/dot_general | solution.py:132
  88.1 1.8 %fusion.82 = bf16[5,64,192]{2,1,0:T(8,128)(2,1)S(1)} fusion(bf16[5,64,192]{2,1,0:T(8,128)(2,1)S(1)} %get-tuple-element.251, s32[]{:T(128)S(6)} %copy.161, bf16[96,5248]{1,0:T(8,128)(2,1)S(1)} %get-tuple-element.234, bf16[96,5248]{1,0:T(8,128)(2,1)S(1)} %get-tuple-element.235, f32[64,5248]{1,0:T(8,128)S(1)} %get-tuple-element.237, ...), kind=kOutput, calls=%fused_computation.15.clone.clone.1 | convolution fusion | flops 134025216 | bytes 4064256 | tf_op jit(solution)/shard_map/while/body/eval_jaxpr/dot_general | solution.py:134
  90.8 1.1 %reshape.465 = bf16[16,2,1920]{2,1,0:T(2,128)(2,1)} reshape(bf16[48,5,2,2,2,32]{5,4,3,2,1,0:T(2,128)(2,1)S(1)} %bitcast.185) | data formatting | bytes 245760
  91.9 3.5 %all-to-all-start.1 = ((bf16[16,2,1920]{2,1,0:T(2,128)(2,1)}), bf16[16,2,1920]{2,1,0:T(2,128)(2,1)S(1)}, u32[]{:S(2)}, u32[]{:S(2)}) async-start(bf16[16,2,1920]{2,1,0:T(2,128)(2,1)} %reshape.465), calls=%async_computation.1 | async-start | bytes 245760 | tf_op jit(solution)/shard_map/all_to_all | solution.py:142
  95.7 7.5 %all-to-all-done.1 = bf16[16,2,1920]{2,1,0:T(2,128)(2,1)S(1)} async-done(((bf16[16,2,1920]{2,1,0:T(2,128)(2,1)}), bf16[16,2,1920]{2,1,0:T(2,128)(2,1)S(1)}, u32[]{:S(2)}, u32[]{:S(2)}) %all-to-all-start.1) | async-done | bytes 122912 | tf_op jit(solution)/shard_map/all_to_all | solution.py:142
  (105 shorter events, 32.2 us)
Async XLA Ops:
  0.6 19.5 %copy-start = (f32[80]{0:T(128)S(1)}, f32[80]{0:T(128)}, u32[]{:S(2)}) copy-start(f32[80]{0:T(128)} %param.11) | copy-start | bytes 964
  24.9 6.5 %copy-start.2 = (s32[5]{0:T(128)S(1)}, s32[5]{0:T(128)}, u32[]{:S(2)}) copy-start(s32[5]{0:T(128)} %param.12) | copy-start | bytes 64
  27.6 11.3 %all-to-all-start = ((bf16[16,2,1920]{2,1,0:T(2,128)(2,1)}), bf16[16,2,1920]{2,1,0:T(2,128)(2,1)S(1)}, u32[]{:S(2)}, u32[]{:S(2)}) async-start(bf16[16,2,1920]{2,1,0:T(2,128)(2,1)} %reshape.463), calls=%async_computation | async-start | bytes 245760 | tf_op jit(solution)/shard_map/all_to_all | solution.py:123
  31.2 8.7 %copy-start.1 = (s32[48,2]{1,0:T(8,128)}, s32[48,2]{1,0:T(8,128)S(1)}, u32[]{:S(2)}) copy-start(s32[48,2]{1,0:T(8,128)S(1)} %copy.99) | copy-start | bytes 1156
  91.9 11.3 %all-to-all-start.1 = ((bf16[16,2,1920]{2,1,0:T(2,128)(2,1)}), bf16[16,2,1920]{2,1,0:T(2,128)(2,1)S(1)}, u32[]{:S(2)}, u32[]{:S(2)}) async-start(bf16[16,2,1920]{2,1,0:T(2,128)(2,1)} %reshape.465), calls=%async_computation.1 | async-start | bytes 245760 | tf_op jit(solution)/shard_map/all_to_all | solution.py:142
where the time goes:
time: 108 us; the launch traced here: 107 us
  other arithmetic  23.5 us (22%)
  local copies, waits for them, and re-layouts  19.3 us (18%)
  matrix products  16.7 us (15%)
  waiting for transfers between devices  15 us (14%)
  blocking collectives  13.7 us (13%)
  loops' own time  9.82 us (9%)
  starting transfers between devices  7.02 us (6%)
  between operations  2.31 us (2%)
    unnamed x1, blocking collectives  13.7 us
    another operation x1, loops' own time, on_device(): fields, returned = lax.map(cycle_step, (received, force_rows, lengths))  9.82 us
    dot_general x5, matrix products, cycle_step(): lax.dot_general(product, dft_table, (((1,), (1,)), ((), ())), preferred_e...  9.21 us
    unnamed x22, local copies, waits for them, and re-layouts  7.76 us
    sub x5, other arithmetic, fourier_table(): cosine = (cos_high * cos_low - sin_high * sin_low).reshape(count, points)  7.68 us
    all_to_all x1, waiting for transfers between devices, on_device(): lax.all_to_all(returned, 'band', split_axis=4, concat_axis=0, tiled=True)  7.54 us
    all_to_all x1, waiting for transfers between devices, on_device(): lax.all_to_all(fourier, 'band', split_axis=0, concat_axis=4, tiled=True)  7.48 us
    dot_general x5, matrix products, cycle_step(): jnp.dot(fourier_cycle, dft_table, preferred_element_type=jnp.float32)  6.83 us
  transfers between devices with their start and end apart: 2, of which 2 were waited for; matrix products, arithmetic and copies ran while one was open for 0% of the time, Pallas kernels for 0%

commit v1 on v0

--- a/solution.py
+++ b/solution.py
@@ -1,8 +1,11 @@
+import functools
 import math
 
 import jax
 import jax.numpy as jnp
 from jax import lax
+from jax.experimental import pallas as pl
+from jax.experimental.pallas import tpu as pltpu
 from jax.sharding import PartitionSpec as P
 
 TRUNC = 1279
@@ -94,7 +97,7 @@
     return merged[:, :, :, : legendre_rows.shape[1]]
 
 
-def on_device(spec_in, forcing, legendre, weights, cycle_slots, wave_pairs):
+def on_device_wide(spec_in, forcing, legendre, weights, cycle_slots, wave_pairs):
     all_cycles, all_pairs = (
         lax.all_gather(cycle_slots, "band", axis=0, tiled=True),
         lax.all_gather(wave_pairs, "band", axis=0, tiled=True),
@@ -153,7 +156,341 @@
     return (grid_field, spec_out)
 
 
+MESH = pl.DeviceIdType.MESH
+BLOCK = 256
+GROUP = 16
+LANES = 128
+
+
+def unit_circle(steps, length, inverse):
+    turns = jnp.floor(steps * inverse + 0.5)
+    z = (steps - turns * length) * (inverse * math.pi)
+    y = z * z
+    s = -1.0 / 39916800.0
+    for c in (1.0 / 362880.0, -1.0 / 5040.0, 1.0 / 120.0, -1.0 / 6.0, 1.0):
+        s = s * y + c
+    s = s * z
+    k = 1.0 / 479001600.0
+    for c in (-1.0 / 3628800.0, 1.0 / 40320.0, -1.0 / 720.0, 1.0 / 24.0, -0.5, 1.0):
+        k = k * y + c
+    return 1.0 - 2.0 * s * s, 2.0 * s * k
+
+
+def fused_kernel(
+    n, slots, lats, levels, lat_count, points,
+    spec_ref, leg_ref, weights_ref, cyc_ref, pair_ref, force_hbm,
+    field_hbm, out_ref,
+    force_v, field_v, info, legm, coefm, send1, recv1, send2, recv2,
+    pick, low, high_c, high_s, coef_z, back_z, twisted, prod,
+    force_sem, field_sem, info_ss, info_rs, f_ss, f_rs, b_ss, b_rs,
+):
+    window = 2 * slots * n
+    row_count = window + 1
+    rows = slots * row_count
+    base = TRUNC + 1 - window
+    pairs = 2 * levels
+    blocks = -(-points // BLOCK)
+    whole = (NLON_EQ - 4 * (lat_count - 1)) // BLOCK
+    f32, bf16, i32 = jnp.float32, jnp.bfloat16, jnp.int32
+    me = lax.axis_index("band")
+    part = lax.axis_index("grp")
+
+    def force_copy(q):
+        return pltpu.make_async_copy(force_hbm.at[q], force_v.at[q], force_sem.at[q])
+
+    def field_copy(q):
+        return pltpu.make_async_copy(field_v.at[q], field_hbm.at[q], field_sem.at[q])
+
+    for q in range(lats):
+        force_copy(q).start()
+
+    barrier = pltpu.get_barrier_semaphore()
+
+    def peer(i):
+        return lax.rem(me + i, n)
+
+    @pl.loop(1, n)
+    def _(i):
+        pl.semaphore_signal(barrier, inc=1, device_id=(part, peer(i)), device_id_type=MESH)
+
+    row16 = lax.broadcasted_iota(i32, (GROUP, LANES), 0)
+    mine = jnp.full((GROUP, LANES), -1, i32)
+    for q in range(lats):
+        for s in range(slots):
+            mine = jnp.where(row16 == q * slots + s, cyc_ref[q] * 65536 + pair_ref[s], mine)
+    info[me] = mine
+
+    def remote(src, dst, ssem, rsem, to, frm):
+        return pltpu.make_async_remote_copy(
+            src_ref=src, dst_ref=dst, send_sem=ssem.at[to], recv_sem=rsem.at[frm],
+            device_id=(part, to), device_id_type=MESH,
+        )
+
+    pl.semaphore_wait(barrier, n - 1)
+
+    @pl.loop(1, n)
+    def _(i):
+        remote(info.at[me], info.at[me], info_ss, info_rs, peer(i), me).start()
+
+    @pl.loop(0, lats)
+    def _(q):
+        length = jnp.full((1, LANES), NLON_EQ - 4 * cyc_ref[q], i32).astype(f32)
+        inverse = 1.0 / length
+        m_low = base + lax.broadcasted_iota(i32, (BLOCK, LANES), 1)
+        v_low = lax.broadcasted_iota(i32, (BLOCK, LANES), 0)
+        c, s = unit_circle((m_low * v_low).astype(f32), length, inverse)
+        low[q, :, 0:LANES] = c.astype(bf16)
+        low[q, :, LANES : 2 * LANES] = s.astype(bf16)
+        height = high_c.shape[1]
+        m_high = base + lax.broadcasted_iota(i32, (height, LANES), 1)
+        u_high = lax.broadcasted_iota(i32, (height, LANES), 0) * BLOCK
+        c, s = unit_circle((m_high * u_high).astype(f32), length, inverse)
+        high_c[q] = c
+        high_s[q] = s
+
+    lane = lax.broadcasted_iota(i32, (1, rows), 1)
+    offset = lane
+    boundary = jnp.full((1, rows), 0, i32) + (window - pair_ref[0])
+    for s in range(1, slots):
+        here = lane >= s * row_count
+        offset = jnp.where(here, lane - s * row_count, offset)
+        boundary = jnp.where(here, window - pair_ref[s], boundary)
+    second = offset >= boundary
+    odd = (jnp.where(second, offset - boundary, offset) & 1) == 1
+    in_wave = [jnp.where(second, 0.0, 1.0), jnp.where(second, 1.0, 0.0)]
+    sign = jnp.where(odd, -1.0, 1.0)
+    for w in range(2):
+        for e in range(2):
+            part_we = spec_ref[e].astype(f32) * in_wave[w]
+            at = (w * 2 + e) * pairs
+            coefm[at : at + levels, :] = part_we.astype(bf16)
+            coefm[at + levels : at + pairs, :] = (part_we * sign).astype(bf16)
+
+    @pl.loop(1, n)
+    def _(i):
+        frm = lax.rem(me + n - i, n)
+        remote(info.at[frm], info.at[frm], info_ss, info_rs, peer(i), frm).wait_recv()
+
+    total = n * GROUP
+    gathered = info[...].reshape(total, LANES)
+    cycles = gathered >> 16
+    waves = gathered & 65535
+    hot = jnp.where(cycles == lax.broadcasted_iota(i32, (total, LANES), 1), 1.0, 0.0)
+    leg_all = lax.dot_general(
+        hot[:, :lat_count].astype(bf16), leg_ref[...], (((1,), (1,)), ((), ())),
+        preferred_element_type=f32,
+    )
+
+    def row_lat(width):
+        place = lax.broadcasted_iota(i32, (total, width), 0) & (GROUP - 1)
+        lat = jnp.zeros((total, width), i32)
+        for k in range(1, GROUP // slots + 1):
+            lat = lat + jnp.where(place >= k * slots, 1, 0)
+        return lat, place - lat * slots
+
+    _, slot_of = row_lat(rows)
+    lane_full = lax.broadcasted_iota(i32, (total, rows), 1) - slot_of * row_count
+    keep = (lane_full >= 0) & (lane_full < row_count)
+    legm[...] = jnp.where(keep, leg_all, 0.0).astype(bf16)
+    fourier = lax.dot_general(
+        legm[...], coefm[...], (((1,), (1,)), ((), ())), preferred_element_type=f32
+    ).astype(bf16)
+    send1[...] = fourier.reshape(n, GROUP, 4 * pairs)
+
+    @pl.loop(1, n)
+    def _(i):
+        remote(send1.at[peer(i)], recv1.at[me], f_ss, f_rs, peer(i), me).start()
+
+    recv1[me] = send1[me]
+    lat_of, _ = row_lat(LANES)
+    lane128 = lax.broadcasted_iota(i32, (total, LANES), 1)
+    for q in range(lats):
+        here = lat_of == q
+        pick[0, q] = jnp.where(here & (lane128 == waves), 1.0, 0.0).astype(bf16)
+        pick[1, q] = jnp.where(here & (lane128 == window - 1 - waves), 1.0, 0.0).astype(bf16)
+
+    @pl.loop(1, n)
+    def _(i):
+        frm = lax.rem(me + n - i, n)
+        remote(send1.at[peer(i)], recv1.at[frm], f_ss, f_rs, peer(i), frm).wait_recv()
+
+    half = 2 * pairs
+    arrived = recv1[...].reshape(total, 2 * half)
+    for q in range(lats):
+        z = jnp.zeros((half, LANES), f32)
+        for w in range(2):
+            z = z + lax.dot_general(
+                arrived[:, w * half : (w + 1) * half], pick[w, q], (((0,), (0,)), ((), ())),
+                preferred_element_type=f32,
+            )
+        coef_z[q] = 2.0 * z
+
+    per = twisted.shape[0] // pairs
+
+    @pl.loop(0, lats)
+    def _(q):
+        force_copy(q).wait()
+        length = NLON_EQ - 4 * cyc_ref[q]
+        acc_re = jnp.zeros((pairs, LANES), f32)
+        acc_im = jnp.zeros((pairs, LANES), f32)
+        for first in range(0, blocks, per):
+            count = min(per, blocks - first)
+            size = count * pairs
+            real = coef_z[q, 0:pairs]
+            imag = coef_z[q, pairs:half]
+            for k in range(count):
+                u = first + k
+                hc = high_c[q, u : u + 1, :]
+                hs = high_s[q, u : u + 1, :]
+                twisted[k * pairs : (k + 1) * pairs, 0:LANES] = (real * hc - imag * hs).astype(bf16)
+                twisted[k * pairs : (k + 1) * pairs, LANES : 2 * LANES] = (
+                    -(real * hs + imag * hc)
+                ).astype(bf16)
+            fields = lax.dot_general(
+                twisted[0:size], low[q], (((1,), (1,)), ((), ())), preferred_element_type=f32
+            )
+            for k in range(count):
+                u = first + k
+                width = min(BLOCK, points - u * BLOCK)
+                f = fields[k * pairs : (k + 1) * pairs, 0:width]
+                if u >= whole:
+                    j = u * BLOCK + lax.broadcasted_iota(i32, (pairs, width), 1)
+                    f = jnp.where(j < length, f, 0.0)
+                field_v[q, :, u * BLOCK : u * BLOCK + width] = f.astype(bf16)
+                p = f * force_v[q, :, u * BLOCK : u * BLOCK + width].astype(f32)
+                prod[k * pairs : (k + 1) * pairs, 0:width] = p.astype(bf16)
+                if width < BLOCK:
+                    prod[k * pairs : (k + 1) * pairs, width:BLOCK] = jnp.zeros(
+                        (pairs, BLOCK - width), bf16
+                    )
+            back = jnp.dot(prod[0:size], low[q], preferred_element_type=f32)
+            for k in range(count):
+                u = first + k
+                hc = high_c[q, u : u + 1, :]
+                hs = high_s[q, u : u + 1, :]
+                tc = back[k * pairs : (k + 1) * pairs, 0:LANES]
+                ts = back[k * pairs : (k + 1) * pairs, LANES : 2 * LANES]
+                acc_re = acc_re + (tc * hc - ts * hs)
+                acc_im = acc_im - (tc * hs + ts * hc)
+        field_copy(q).start()
+        weight = weights_ref[cyc_ref[q]]
+        for e, acc in ((0, acc_re), (1, acc_im)):
+            rounded = acc.astype(bf16).astype(f32)
+            north = rounded[0:levels]
+            south = rounded[levels:pairs]
+            back_z[q, e * pairs : e * pairs + levels] = (weight * (north + south)).astype(bf16)
+            back_z[q, e * pairs + levels : (e + 1) * pairs] = (weight * (north - south)).astype(bf16)
+
+    for w in range(2):
+        z = jnp.zeros((total, half), f32)
+        for q in range(lats):
+            z = z + lax.dot_general(
+                pick[w, q], back_z[q], (((1,), (1,)), ((), ())), preferred_element_type=f32
+            )
+        send2[:, :, w * half : (w + 1) * half] = z.astype(bf16).reshape(n, GROUP, half)
+
+    @pl.loop(1, n)
+    def _(i):
+        remote(send2.at[peer(i)], recv2.at[me], b_ss, b_rs, peer(i), me).start()
+
+    recv2[me] = send2[me]
+
+    @pl.loop(1, n)
+    def _(i):
+        frm = lax.rem(me + n - i, n)
+        remote(send2.at[peer(i)], recv2.at[frm], b_ss, b_rs, peer(i), frm).wait_recv()
+
+    final = lax.dot_general(
+        recv2[...].reshape(total, 2 * half), legm[...], (((0,), (0,)), ((), ())),
+        preferred_element_type=f32,
+    )
+    for e in range(2):
+        chosen = []
+        for w in range(2):
+            at = (w * 2 + e) * pairs
+            chosen.append(
+                jnp.where(odd, final[at + levels : at + pairs], final[at : at + levels])
+            )
+        out_ref[e] = jnp.where(second, chosen[1], chosen[0])
+
+    @pl.loop(1, n)
+    def _(i):
+        to = peer(i)
+        remote(info.at[me], info.at[me], info_ss, info_rs, to, me).wait_send()
+        remote(send1.at[to], recv1.at[me], f_ss, f_rs, to, me).wait_send()
+        remote(send2.at[to], recv2.at[me], b_ss, b_rs, to, me).wait_send()
+
+    for q in range(lats):
+        field_copy(q).wait()
+
+
+def on_device(n, spec_in, forcing, legendre, weights, cycle_slots, wave_pairs):
+    slots = wave_pairs.shape[0]
+    lats = cycle_slots.shape[0]
+    levels = spec_in.shape[1]
+    rows, lat_count = legendre.shape
+    points = forcing.shape[3]
+    pairs = 2 * levels
+    half = 2 * pairs
+    total = n * GROUP
+    blocks = -(-points // BLOCK)
+    per = 7
+    bf16, f32 = jnp.bfloat16, jnp.float32
+    vmem = pl.BlockSpec(memory_space=pltpu.VMEM)
+    smem = pl.BlockSpec(memory_space=pltpu.SMEM)
+    hbm = pl.BlockSpec(memory_space=pl.ANY)
+    dma = pltpu.SemaphoreType.DMA
+    high_rows = -(-blocks // 8) * 8
+    field, spec_out = pl.pallas_call(
+        functools.partial(fused_kernel, n, slots, lats, levels, lat_count, points),
+        out_shape=(
+            jax.ShapeDtypeStruct((lats, pairs, points), bf16),
+            jax.ShapeDtypeStruct((2, levels, rows), f32),
+        ),
+        in_specs=[vmem, vmem, smem, smem, smem, hbm],
+        out_specs=(hbm, vmem),
+        scratch_shapes=[
+            pltpu.VMEM((lats, pairs, points), bf16),
+            pltpu.VMEM((lats, pairs, points), bf16),
+            pltpu.VMEM((n, GROUP, LANES), jnp.int32),
+            pltpu.VMEM((total, rows), bf16),
+            pltpu.VMEM((2 * half, rows), bf16),
+            pltpu.VMEM((n, GROUP, 2 * half), bf16),
+            pltpu.VMEM((n, GROUP, 2 * half), bf16),
+            pltpu.VMEM((n, GROUP, 2 * half), bf16),
+            pltpu.VMEM((n, GROUP, 2 * half), bf16),
+            pltpu.VMEM((2, lats, total, LANES), bf16),
+            pltpu.VMEM((lats, BLOCK, 2 * LANES), bf16),
+            pltpu.VMEM((lats, high_rows, LANES), f32),
+            pltpu.VMEM((lats, high_rows, LANES), f32),
+            pltpu.VMEM((lats, half, LANES), f32),
+            pltpu.VMEM((lats, half, LANES), bf16),
+            pltpu.VMEM((per * pairs, 2 * LANES), bf16),
+            pltpu.VMEM((per * pairs, 2 * LANES), bf16),
+            dma((lats,)), dma((lats,)),
+            dma((n,)), dma((n,)), dma((n,)), dma((n,)), dma((n,)), dma((n,)),
+        ],
+        compiler_params=pltpu.CompilerParams(
+            collective_id=0, has_side_effects=True, vmem_limit_bytes=48 * 1024 * 1024
+        ),
+    )(spec_in, legendre, weights, cycle_slots, wave_pairs, forcing.reshape(lats, pairs, points))
+    return field.reshape(lats, 2, levels, points), spec_out
+
+
 def solution(mesh):
+    n = mesh.shape["band"]
+
+    def run(spec_in, forcing, legendre, weights, cycle_slots, wave_pairs):
+        slots = wave_pairs.shape[0]
+        narrow = (
+            2 * slots * n <= LANES
+            and legendre.shape[1] <= LANES
+            and slots * cycle_slots.shape[0] <= GROUP
+            and spec_in.shape[1] % 32 == 0
+        )
+        args = (spec_in, forcing, legendre, weights, cycle_slots, wave_pairs)
+        return on_device(n, *args) if narrow else on_device_wide(*args)
+
     in_specs = (
         P(None, "grp", "band"),
         P("band", None, "grp", None),
@@ -164,5 +501,5 @@
     )
     out_specs = (P("band", None, "grp", None), P(None, "grp", "band"))
     return jax.shard_map(
-        on_device, mesh=mesh, in_specs=in_specs, out_specs=out_specs, check_vma=False
-    )
+        run, mesh=mesh, in_specs=in_specs, out_specs=out_specs, check_vma=False
+    )

time: 108 us -> 35.9 us (0.33)
  Pallas kernels: 0 us -> 28.9 us
  other arithmetic: 23.5 us -> 0 us
  matrix products: 16.7 us -> 0 us
  waiting for transfers between devices: 15 us -> 0 us
  blocking collectives: 13.7 us -> 0 us
  local copies, waits for them, and re-layouts: 19.3 us -> 6.08 us
  loops' own time: 9.82 us -> 0 us
  starting transfers between devices: 7.02 us -> 0 us
  between operations: 2.31 us -> 0.65 us
    pallas_call x0 -> x1, Pallas kernels: none -> 28.9 us  [on_device(): pl.pallas_call(functools.partial(fused_kernel, n, slots, lats, levels, la...]
    dot_general x14 -> x0, matrix products: 16.7 us -> none  [the longest x5 9.21 us: cycle_step(): lax.dot_general(product, dft_table, (((1,), (1,)), ((), ())), preferred_e...]
    all_to_all x2 -> x0, waiting for transfers between devices: 15 us -> none  [the longest x1 7.54 us: on_device(): lax.all_to_all(returned, 'band', split_axis=4, concat_axis=0, tiled=True)]
    unnamed x1 -> x0, blocking collectives: 13.7 us -> none
    another operation x1 -> x0, loops' own time: 9.82 us -> none  [on_device(): fields, returned = lax.map(cycle_step, (received, force_rows, lengths))]
    sub x7 -> x0, other arithmetic: 8.34 us -> none  [the longest x5 7.68 us: fourier_table(): cosine = (cos_high * cos_low - sin_high * sin_low).reshape(count, points)]
    cos x10 -> x0, other arithmetic: 7.71 us -> none  [the longest x5 3.86 us: fourier_table(): cos_high = jnp.cos(angle_high)[:, :, None]]
    all_to_all x2 -> x0, starting transfers between devices: 7.02 us -> none  [the longest x1 3.51 us: on_device(): lax.all_to_all(fourier, 'band', split_axis=0, concat_axis=4, tiled=True)]
  transfers between devices with their start and end apart: 2 -> 0, of which waited for: 2 -> 0; matrix products, arithmetic and copies ran while one was open for 0% -> 0% of each run, Pallas kernels for 0% -> 0%
where the time goes in v1:
time: 35.9 us; the launch traced here: 35.6 us
  Pallas kernels  28.9 us (81%)
  local copies, waits for them, and re-layouts  6.08 us (17%)
  between operations  0.65 us (2%)
    pallas_call x1, Pallas kernels, on_device(): pl.pallas_call(functools.partial(fused_kernel, n, slots, lats, levels, la...  28.9 us
    unnamed x11, local copies, waits for them, and re-layouts  6.08 us

profile of v1, /device:TPU:0, one launch (start us, length us, event | category | flops | bytes accessed | tf_op | source)
XLA Modules:
  0.0 35.6 jit_solution(10190832970905220361)
XLA Ops:
  0.6 0.9 %copy.8.leg_ref = bf16[291,80]{1,0:T(8,128)(2,1)S(1)} copy(bf16[291,80]{0,1:T(8,128)(2,1)} %param.8) | data formatting | bytes 93120 | tf_op args[2]
  1.6 0.0 copy-start
  1.6 0.8 %copy-done = bf16[2,32,291]{2,1,0:T(8,128)(2,1)S(1)} copy-done((bf16[2,32,291]{2,1,0:T(8,128)(2,1)S(1)}, bf16[2,32,291]{2,1,0:T(8,128)(2,1)}, u32[]{:S(2)}) %copy-start) | copy-done | bytes 37272
  2.4 0.0 copy-start.1
  2.4 0.7 %copy-done.1 = f32[80]{0:T(128)S(1)} copy-done((f32[80]{0:T(128)S(1)}, f32[80]{0:T(128)}, u32[]{:S(2)}) %copy-start.1) | copy-done | bytes 344
  3.0 0.0 copy-start.2
  3.0 0.7 %copy-done.2 = s32[5]{0:T(128)S(1)} copy-done((s32[5]{0:T(128)S(1)}, s32[5]{0:T(128)}, u32[]{:S(2)}) %copy-start.2) | copy-done | bytes 44
  3.7 0.0 copy-start.3
  3.7 0.7 %copy-done.3 = s32[3]{0:T(128)S(1)} copy-done((s32[3]{0:T(128)S(1)}, s32[3]{0:T(128)}, u32[]{:S(2)}) %copy-start.3) | copy-done | bytes 36
  4.4 28.9 %shard_map.77 = (bf16[5,64,5248]{2,1,0:T(8,128)(2,1)S(1)}, f32[2,32,291]{2,1,0:T(8,128)S(1)}) custom-call(bf16[2,32,291]{2,1,0:T(8,128)(2,1)S(1)} %copy-done, bf16[291,80]{1,0:T(8,128)(2,1)S(1)} %copy.8.leg_ref, f32[80]{0:T(128)S(1)} %copy-done.1, s32[5]{0:T(128)S(1)} %copy-done.2, s32[3]{0:T(128)S(1)} %copy-done.3, bf16[5,64,5248]{2,1,0:T(8,128)(2,1)} %bitcast.3), custom_call_target="tpu_custom_call" | custom-call | tf_op jit(solution)/shard_map/pallas_call | solution.py:444
  33.2 1.7 %copy.11 = bf16[5,2,32,5248]{3,2,1,0:T(8,128)(2,1)} copy(bf16[5,2,32,5248]{3,2,1,0:T(8,128)(2,1)S(1)} %bitcast.2) | data formatting | bytes 6717440
  35.0 0.6 %copy.12 = f32[2,32,291]{2,1,0:T(8,128)} copy(f32[2,32,291]{2,1,0:T(8,128)S(1)} %get-tuple-element.9) | data formatting | bytes 148992
Async XLA Ops:
  1.6 0.8 %copy-start = (bf16[2,32,291]{2,1,0:T(8,128)(2,1)S(1)}, bf16[2,32,291]{2,1,0:T(8,128)(2,1)}, u32[]{:S(2)}) copy-start(bf16[2,32,291]{2,1,0:T(8,128)(2,1)} %spec_ref.1) | copy-start | bytes 111748
  2.4 0.7 %copy-start.1 = (f32[80]{0:T(128)S(1)}, f32[80]{0:T(128)}, u32[]{:S(2)}) copy-start(f32[80]{0:T(128)} %weights_ref.1) | copy-start | bytes 964
  3.0 0.7 %copy-start.2 = (s32[5]{0:T(128)S(1)}, s32[5]{0:T(128)}, u32[]{:S(2)}) copy-start(s32[5]{0:T(128)} %cyc_ref.1) | copy-start | bytes 64
  3.7 0.7 %copy-start.3 = (s32[3]{0:T(128)S(1)}, s32[3]{0:T(128)}, u32[]{:S(2)}) copy-start(s32[3]{0:T(128)} %pair_ref.1) | copy-start | bytes 40

commit v2 on v0

--- a/solution.py
+++ b/solution.py
@@ -1,8 +1,11 @@
+import functools
 import math
 
 import jax
 import jax.numpy as jnp
 from jax import lax
+from jax.experimental import pallas as pl
+from jax.experimental.pallas import tpu as pltpu
 from jax.sharding import PartitionSpec as P
 
 TRUNC = 1279
@@ -94,7 +97,7 @@
     return merged[:, :, :, : legendre_rows.shape[1]]
 
 
-def on_device(spec_in, forcing, legendre, weights, cycle_slots, wave_pairs):
+def on_device_wide(spec_in, forcing, legendre, weights, cycle_slots, wave_pairs):
     all_cycles, all_pairs = (
         lax.all_gather(cycle_slots, "band", axis=0, tiled=True),
         lax.all_gather(wave_pairs, "band", axis=0, tiled=True),
@@ -153,7 +156,398 @@
     return (grid_field, spec_out)
 
 
+MESH = pl.DeviceIdType.MESH
+BLOCK = 256
+GROUP = 16
+CHUNKS = 1
+PER = 21
+LANES = 128
+
+
+def unit_circle(steps, length, inverse):
+    turns = jnp.floor(steps * inverse + 0.5)
+    z = (steps - turns * length) * (inverse * math.pi)
+    y = z * z
+    s = -1.0 / 39916800.0
+    for c in (1.0 / 362880.0, -1.0 / 5040.0, 1.0 / 120.0, -1.0 / 6.0, 1.0):
+        s = s * y + c
+    s = s * z
+    k = 1.0 / 479001600.0
+    for c in (-1.0 / 3628800.0, 1.0 / 40320.0, -1.0 / 720.0, 1.0 / 24.0, -0.5, 1.0):
+        k = k * y + c
+    return 1.0 - 2.0 * s * s, 2.0 * s * k
+
+
+def fused_kernel(
+    n, slots, lats, levels, lat_count, points,
+    spec_hbm, leg_hbm, weights_hbm, cyc_hbm, pair_hbm, force_hbm,
+    field_v, out_ref,
+    spec_ref, leg_ref, weights_ref, cyc_ref, pair_ref, small_sem, force_v, info, legm, coefm, send1, recv1, send2, recv2,
+    pick, low, high_c, high_s, coef_z, back_z, twisted, prod,
+    force_sem, info_ss, info_rs, f_ss, f_rs, b_ss, b_rs,
+):
+    window = 2 * slots * n
+    row_count = window + 1
+    rows = slots * row_count
+    base = TRUNC + 1 - window
+    chunks = send1.shape[0]
+    part_levels = levels // chunks
+    pairs = 2 * part_levels
+    half = 2 * pairs
+    blocks = -(-points // BLOCK)
+    whole = (NLON_EQ - 4 * (lat_count - 1)) // BLOCK
+    f32, bf16, i32 = jnp.float32, jnp.bfloat16, jnp.int32
+    me = lax.axis_index("band")
+    part = lax.axis_index("grp")
+
+    def force_copy(q):
+        return pltpu.make_async_copy(force_hbm.at[q], force_v.at[q], force_sem.at[q])
+
+    small = [
+        pltpu.make_async_copy(a, b, small_sem.at[i])
+        for i, (a, b) in enumerate(
+            (
+                (cyc_hbm, cyc_ref),
+                (pair_hbm, pair_ref),
+                (spec_hbm, spec_ref),
+                (leg_hbm, leg_ref),
+                (weights_hbm, weights_ref),
+            )
+        )
+    ]
+    for copy in small:
+        copy.start()
+
+    barrier = pltpu.get_barrier_semaphore()
+
+    def peer(i):
+        return lax.rem(me + i, n)
+
+    @pl.loop(1, n)
+    def _(i):
+        pl.semaphore_signal(barrier, inc=1, device_id=(part, peer(i)), device_id_type=MESH)
+
+    for q in range(lats):
+        force_copy(q).start()
+    small[0].wait()
+    small[1].wait()
+
+    lane1 = lax.broadcasted_iota(i32, (1, LANES), 1)
+    mine = jnp.full((1, LANES), -1.0, f32)
+    for q in range(lats):
+        for s in range(slots):
+            k = q * slots + s
+            mine = jnp.where(lane1 == k, cyc_ref[q].astype(f32), mine)
+            mine = jnp.where(lane1 == GROUP + k, pair_ref[s].astype(f32), mine)
+    info[me] = mine
+
+    def remote(src, dst, ssem, rsem, to):
+        return pltpu.make_async_remote_copy(
+            src_ref=src, dst_ref=dst, send_sem=ssem, recv_sem=rsem,
+            device_id=(part, to), device_id_type=MESH,
+        )
+
+    def all_of(buffer, sem):
+        others = buffer.at[pl.ds(0, n - 1)]
+        return pltpu.make_async_copy(others, others, sem)
+
+    pl.semaphore_wait(barrier, n - 1)
+
+    @pl.loop(1, n)
+    def _(i):
+        remote(info.at[me], info.at[me], info_ss.at[0], info_rs.at[0], peer(i)).start()
+
+    @pl.loop(0, lats)
+    def _(q):
+        length = jnp.full((1, LANES), NLON_EQ - 4 * cyc_ref[q], i32).astype(f32)
+        inverse = 1.0 / length
+        m_low = base + lax.broadcasted_iota(i32, (BLOCK, LANES), 1)
+        v_low = lax.broadcasted_iota(i32, (BLOCK, LANES), 0)
+        c, s = unit_circle((m_low * v_low).astype(f32), length, inverse)
+        low[q, :, 0:LANES] = c.astype(bf16)
+        low[q, :, LANES : 2 * LANES] = s.astype(bf16)
+        height = high_c.shape[1]
+        m_high = base + lax.broadcasted_iota(i32, (height, LANES), 1)
+        u_high = lax.broadcasted_iota(i32, (height, LANES), 0) * BLOCK
+        c, s = unit_circle((m_high * u_high).astype(f32), length, inverse)
+        high_c[q] = c
+        high_s[q] = s
+
+    for copy in small[2:]:
+        copy.wait()
+
+    lane = lax.broadcasted_iota(i32, (1, rows), 1)
+    offset = lane
+    boundary = jnp.full((1, rows), 0, i32) + (window - pair_ref[0])
+    for s in range(1, slots):
+        here = lane >= s * row_count
+        offset = jnp.where(here, lane - s * row_count, offset)
+        boundary = jnp.where(here, window - pair_ref[s], boundary)
+    second = offset >= boundary
+    odd = (jnp.where(second, offset - boundary, offset) & 1) == 1
+    in_wave = [jnp.where(second, 0.0, 1.0), jnp.where(second, 1.0, 0.0)]
+    sign = jnp.where(odd, -1.0, 1.0)
+    for e in range(2):
+        values = spec_ref[e].astype(f32)
+        for w in range(2):
+            north = values * in_wave[w]
+            south = north * sign
+            for c in range(chunks):
+                at = c * 2 * half + (w * 2 + e) * pairs
+                take = slice(c * part_levels, (c + 1) * part_levels)
+                coefm[at : at + part_levels, :] = north[take].astype(bf16)
+                coefm[at + part_levels : at + pairs, :] = south[take].astype(bf16)
+    back_z[...] = jnp.zeros_like(back_z)
+    all_of(info, info_rs.at[0]).wait()
+
+    total = n * GROUP
+    gathered = jnp.broadcast_to(info[...], (n, GROUP, LANES)).reshape(total, LANES)
+    lane_all = lax.broadcasted_iota(i32, (total, LANES), 1)
+    place_all = lax.broadcasted_iota(i32, (total, LANES), 0) & (GROUP - 1)
+
+    def column(first):
+        here = lane_all == place_all + first
+        return jnp.sum(jnp.where(here, gathered, 0.0), axis=1, keepdims=True).astype(i32)
+
+    cycles = column(0)
+    waves = column(GROUP)
+    hot = jnp.where(cycles == lax.broadcasted_iota(i32, (total, LANES), 1), 1.0, 0.0)
+    leg_all = lax.dot_general(
+        hot[:, :lat_count].astype(bf16), leg_ref[...], (((1,), (0,)), ((), ())),
+        preferred_element_type=f32,
+    )
+
+    def row_lat(width):
+        place = lax.broadcasted_iota(i32, (total, width), 0) & (GROUP - 1)
+        lat = jnp.zeros((total, width), i32)
+        for k in range(1, GROUP // slots + 1):
+            lat = lat + jnp.where(place >= k * slots, 1, 0)
+        return lat, place - lat * slots
+
+    _, slot_of = row_lat(rows)
+    lane_full = lax.broadcasted_iota(i32, (total, rows), 1) - slot_of * row_count
+    keep = (lane_full >= 0) & (lane_full < row_count)
+    legm[...] = jnp.where(keep, leg_all, 0.0).astype(bf16)
+    fourier = lax.dot_general(
+        legm[...], coefm[...], (((1,), (1,)), ((), ())), preferred_element_type=f32
+    ).astype(bf16)
+    for c in range(chunks):
+        send1[c] = fourier[:, c * 2 * half : (c + 1) * 2 * half].reshape(n, GROUP, 2 * half)
+
+    for c in range(chunks):
+
+        @pl.loop(1, n)
+        def _(i):
+            to = peer(i)
+            remote(send1.at[c, to], recv1.at[c, me], f_ss.at[c], f_rs.at[c], to).start()
+
+        recv1[c, me] = send1[c, me]
+
+    lat_of, _ = row_lat(LANES)
+    for q in range(lats):
+        here = lat_of == q
+        at = q * 2 * LANES
+        pick[:, at : at + LANES] = jnp.where(here & (lane_all == waves), 1.0, 0.0).astype(bf16)
+        pick[:, at + LANES : at + 2 * LANES] = jnp.where(
+            here & (lane_all == window - 1 - waves), 1.0, 0.0
+        ).astype(bf16)
+
+    per = twisted.shape[0] // pairs
+    for c in range(chunks):
+
+        all_of(recv1.at[c], f_rs.at[c]).wait()
+
+        arrived = recv1[c].reshape(total, 2 * half)
+        both = lax.dot_general(
+            arrived, pick[...], (((0,), (0,)), ((), ())), preferred_element_type=f32
+        )
+        for q in range(lats):
+            at = q * 2 * LANES
+            coef_z[c, q] = 2.0 * (
+                both[0:half, at : at + LANES] + both[half : 2 * half, at + LANES : at + 2 * LANES]
+            )
+
+        @pl.loop(0, lats)
+        def _(q):
+            if c == 0:
+                force_copy(q).wait()
+            length = NLON_EQ - 4 * cyc_ref[q]
+            acc_re = jnp.zeros((pairs, LANES), f32)
+            acc_im = jnp.zeros((pairs, LANES), f32)
+            for first in range(0, blocks, per):
+                count = min(per, blocks - first)
+                fields = low_sums(coef_z, high_c, high_s, low, twisted, (c, q), q, pairs, first, count)
+                for k in range(count):
+                    u = first + k
+                    width = min(BLOCK, points - u * BLOCK)
+                    f = inside(fields[k * pairs : (k + 1) * pairs, 0:width], u, whole, length)
+                    cols = slice(u * BLOCK, u * BLOCK + width)
+                    for h in range(2):
+                        rows_h = slice(h * levels + c * part_levels, h * levels + (c + 1) * part_levels)
+                        at = k * pairs + h * part_levels
+                        fh = f[h * part_levels : (h + 1) * part_levels]
+                        field_v[q, rows_h, cols] = fh.astype(bf16)
+                        p = fh * force_v[q, rows_h, cols].astype(f32)
+                        prod[at : at + part_levels, 0:width] = p.astype(bf16)
+                    if width < BLOCK:
+                        prod[k * pairs : (k + 1) * pairs, width:BLOCK] = jnp.zeros(
+                            (pairs, BLOCK - width), bf16
+                        )
+                back = jnp.dot(prod[0 : count * pairs], low[q], preferred_element_type=f32)
+                for k in range(count):
+                    u = first + k
+                    hc = high_c[q, u : u + 1, :]
+                    hs = high_s[q, u : u + 1, :]
+                    tc = back[k * pairs : (k + 1) * pairs, 0:LANES]
+                    ts = back[k * pairs : (k + 1) * pairs, LANES : 2 * LANES]
+                    acc_re = acc_re + (tc * hc - ts * hs)
+                    acc_im = acc_im - (tc * hs + ts * hc)
+            weight = weights_ref[cyc_ref[q]]
+            for e, acc in ((0, acc_re), (1, acc_im)):
+                rounded = acc.astype(bf16).astype(f32)
+                north = rounded[0:part_levels]
+                south = rounded[part_levels:pairs]
+                for g, value in ((0, north + south), (1, north - south)):
+                    value = (weight * value).astype(bf16)
+                    for w in range(2):
+                        at = w * half + e * pairs + g * part_levels
+                        lane_at = pl.multiple_of(q * 2 * LANES + w * LANES, LANES)
+                        back_z[at : at + part_levels, pl.ds(lane_at, LANES)] = value
+
+        z = lax.dot_general(
+            pick[...], back_z[...], (((1,), (1,)), ((), ())), preferred_element_type=f32
+        )
+        send2[c] = z.astype(bf16).reshape(n, GROUP, 2 * half)
+
+        @pl.loop(1, n)
+        def _(i):
+            to = peer(i)
+            remote(send2.at[c, to], recv2.at[c, me], b_ss.at[c], b_rs.at[c], to).start()
+
+        recv2[c, me] = send2[c, me]
+
+    for c in range(chunks):
+
+        all_of(recv2.at[c], b_rs.at[c]).wait()
+
+        final = lax.dot_general(
+            recv2[c].reshape(total, 2 * half), legm[...], (((0,), (0,)), ((), ())),
+            preferred_element_type=f32,
+        )
+        for e in range(2):
+            chosen = []
+            for w in range(2):
+                at = (w * 2 + e) * pairs
+                chosen.append(
+                    jnp.where(odd, final[at + part_levels : at + pairs], final[at : at + part_levels])
+                )
+            out_ref[e, c * part_levels : (c + 1) * part_levels] = jnp.where(second, chosen[1], chosen[0])
+
+    all_of(info, info_ss.at[0]).wait()
+    for c in range(chunks):
+        all_of(send1.at[c], f_ss.at[c]).wait()
+        all_of(send2.at[c], b_ss.at[c]).wait()
+
+
+def low_sums(coef_z, high_c, high_s, low, twisted, at, q, pairs, first, count):
+    real = coef_z[at[0], at[1], 0:pairs]
+    imag = coef_z[at[0], at[1], pairs : 2 * pairs]
+    for k in range(count):
+        hc = high_c[q, first + k : first + k + 1, :]
+        hs = high_s[q, first + k : first + k + 1, :]
+        rows = slice(k * pairs, (k + 1) * pairs)
+        twisted[rows, 0:LANES] = (real * hc - imag * hs).astype(jnp.bfloat16)
+        twisted[rows, LANES : 2 * LANES] = (-(real * hs + imag * hc)).astype(jnp.bfloat16)
+    return lax.dot_general(
+        twisted[0 : count * pairs], low[q], (((1,), (1,)), ((), ())),
+        preferred_element_type=jnp.float32,
+    )
+
+
+def inside(f, u, whole, length):
+    if u < whole:
+        return f
+    j = u * BLOCK + lax.broadcasted_iota(jnp.int32, f.shape, 1)
+    return jnp.where(j < length, f, 0.0)
+
+
+def on_device(n, spec_in, forcing, legendre, weights, cycle_slots, wave_pairs):
+    slots = wave_pairs.shape[0]
+    lats = cycle_slots.shape[0]
+    levels = spec_in.shape[1]
+    rows, lat_count = legendre.shape
+    points = forcing.shape[3]
+    chunks = CHUNKS
+    pairs = 2 * levels // chunks
+    half = 2 * pairs
+    total = n * GROUP
+    blocks = -(-points // BLOCK)
+    per = PER
+    bf16, f32 = jnp.bfloat16, jnp.float32
+    vmem = pl.BlockSpec(memory_space=pltpu.VMEM)
+    hbm = pl.BlockSpec(memory_space=pltpu.HBM)
+    dma = pltpu.SemaphoreType.DMA
+    high_rows = -(-blocks // 8) * 8
+    coef_shape = (chunks, lats, half, LANES)
+    low_shape = (lats, BLOCK, 2 * LANES)
+    high_shape = (lats, high_rows, LANES)
+    message = pltpu.VMEM((chunks, n, GROUP, 2 * half), bf16)
+    field, spec_out = pl.pallas_call(
+        functools.partial(fused_kernel, n, slots, lats, levels, lat_count, points),
+        out_shape=(
+            jax.ShapeDtypeStruct((lats, 2 * levels, points), bf16),
+            jax.ShapeDtypeStruct((2, levels, rows), f32),
+        ),
+        in_specs=[hbm] * 6,
+        out_specs=(vmem, vmem),
+        scratch_shapes=[
+            pltpu.VMEM((2, levels, rows), bf16),
+            pltpu.VMEM((lat_count, rows), bf16),
+            pltpu.SMEM((lat_count,), f32),
+            pltpu.SMEM((lats,), jnp.int32),
+            pltpu.SMEM((slots,), jnp.int32),
+            dma((5,)),
+            pltpu.VMEM((lats, 2 * levels, points), bf16),
+            pltpu.VMEM((n, 1, LANES), f32),
+            pltpu.VMEM((total, rows), bf16),
+            pltpu.VMEM((chunks * 2 * half, rows), bf16),
+            message, message, message, message,
+            pltpu.VMEM((total, lats * 2 * LANES), bf16),
+            pltpu.VMEM(low_shape, bf16),
+            pltpu.VMEM(high_shape, f32),
+            pltpu.VMEM(high_shape, f32),
+            pltpu.VMEM(coef_shape, f32),
+            pltpu.VMEM((2 * half, lats * 2 * LANES), bf16),
+            pltpu.VMEM((per * pairs, 2 * LANES), bf16),
+            pltpu.VMEM((per * pairs, 2 * LANES), bf16),
+            dma((lats,)), dma((1,)), dma((1,)),
+            dma((chunks,)), dma((chunks,)), dma((chunks,)), dma((chunks,)),
+        ],
+        compiler_params=pltpu.CompilerParams(
+            collective_id=0, has_side_effects=True,
+            vmem_limit_bytes=49 * 1024 * 1024 + 512 * 1024,
+        ),
+    )(
+        spec_in, legendre.T, weights, cycle_slots, wave_pairs,
+        forcing.reshape(lats, 2 * levels, points),
+    )
+    return field.reshape(lats, 2, levels, points), spec_out
+
+
 def solution(mesh):
+    n = mesh.shape["band"]
+
+    def run(spec_in, forcing, legendre, weights, cycle_slots, wave_pairs):
+        slots = wave_pairs.shape[0]
+        narrow = (
+            2 * slots * n <= LANES
+            and legendre.shape[1] <= LANES
+            and slots * cycle_slots.shape[0] <= GROUP
+            and spec_in.shape[1] % 32 == 0
+        )
+        args = (spec_in, forcing, legendre, weights, cycle_slots, wave_pairs)
+        return on_device(n, *args) if narrow else on_device_wide(*args)
+
     in_specs = (
         P(None, "grp", "band"),
         P("band", None, "grp", None),
@@ -164,5 +558,5 @@
     )
     out_specs = (P("band", None, "grp", None), P(None, "grp", "band"))
     return jax.shard_map(
-        on_device, mesh=mesh, in_specs=in_specs, out_specs=out_specs, check_vma=False
-    )
+        run, mesh=mesh, in_specs=in_specs, out_specs=out_specs, check_vma=False
+    )

time: 108 us -> 30.5 us (0.28)
  Pallas kernels: 0 us -> 23.6 us
  other arithmetic: 23.5 us -> 0 us
  matrix products: 16.7 us -> 0 us
  waiting for transfers between devices: 15 us -> 0 us
  blocking collectives: 13.7 us -> 0 us
  local copies, waits for them, and re-layouts: 19.3 us -> 5.96 us
  loops' own time: 9.82 us -> 0 us
  starting transfers between devices: 7.02 us -> 0 us
  between operations: 2.31 us -> 0.65 us
    pallas_call x0 -> x1, Pallas kernels: none -> 23.6 us  [on_device(): pl.pallas_call(functools.partial(fused_kernel, n, slots, lats, levels, la...]
    dot_general x14 -> x0, matrix products: 16.7 us -> none  [the longest x5 9.21 us: cycle_step(): lax.dot_general(product, dft_table, (((1,), (1,)), ((), ())), preferred_e...]
    all_to_all x2 -> x0, waiting for transfers between devices: 15 us -> none  [the longest x1 7.54 us: on_device(): lax.all_to_all(returned, 'band', split_axis=4, concat_axis=0, tiled=True)]
    unnamed x1 -> x0, blocking collectives: 13.7 us -> none
    another operation x1 -> x0, loops' own time: 9.82 us -> none  [on_device(): fields, returned = lax.map(cycle_step, (received, force_rows, lengths))]
    sub x7 -> x0, other arithmetic: 8.34 us -> none  [the longest x5 7.68 us: fourier_table(): cosine = (cos_high * cos_low - sin_high * sin_low).reshape(count, points)]
    cos x10 -> x0, other arithmetic: 7.71 us -> none  [the longest x5 3.86 us: fourier_table(): cos_high = jnp.cos(angle_high)[:, :, None]]
    all_to_all x2 -> x0, starting transfers between devices: 7.02 us -> none  [the longest x1 3.51 us: on_device(): lax.all_to_all(fourier, 'band', split_axis=0, concat_axis=4, tiled=True)]
  transfers between devices with their start and end apart: 2 -> 0, of which waited for: 2 -> 0; matrix products, arithmetic and copies ran while one was open for 0% -> 0% of each run, Pallas kernels for 0% -> 0%
where the time goes in v2:
time: 30.5 us; the launch traced here: 30.2 us
  Pallas kernels  23.6 us (77%)
  local copies, waits for them, and re-layouts  5.96 us (20%)
  between operations  0.65 us (2%)
    pallas_call x1, Pallas kernels, on_device(): pl.pallas_call(functools.partial(fused_kernel, n, slots, lats, levels, la...  23.6 us
    unnamed x12, local copies, waits for them, and re-layouts  5.96 us

profile of v2, /device:TPU:0, one launch (start us, length us, event | category | flops | bytes accessed | tf_op | source)
XLA Modules:
  0.0 30.2 jit_solution(13676502260238147027)
XLA Ops:
  0.6 0.0 copy-start
  0.6 0.8 %copy-done = bf16[291,80]{0,1:T(8,128)(2,1)S(1)} copy-done((bf16[291,80]{0,1:T(8,128)(2,1)S(1)}, bf16[291,80]{0,1:T(8,128)(2,1)}, u32[]{:S(2)}) %copy-start) | copy-done | bytes 46584
  1.5 0.0 copy-start.1
  1.5 0.8 %copy-done.1 = bf16[2,32,291]{2,1,0:T(8,128)(2,1)S(1)} copy-done((bf16[2,32,291]{2,1,0:T(8,128)(2,1)S(1)}, bf16[2,32,291]{2,1,0:T(8,128)(2,1)}, u32[]{:S(2)}) %copy-start.1) | copy-done | bytes 37272
  2.3 0.0 copy-start.2
  2.3 0.7 %copy-done.2 = f32[80]{0:T(128)S(1)} copy-done((f32[80]{0:T(128)S(1)}, f32[80]{0:T(128)}, u32[]{:S(2)}) %copy-start.2) | copy-done | bytes 344
  2.9 0.0 copy-start.3
  2.9 0.7 %copy-done.3 = s32[5]{0:T(128)S(1)} copy-done((s32[5]{0:T(128)S(1)}, s32[5]{0:T(128)}, u32[]{:S(2)}) %copy-start.3) | copy-done | bytes 44
  3.6 0.0 copy-start.4
  3.6 0.7 %copy-done.4 = s32[3]{0:T(128)S(1)} copy-done((s32[3]{0:T(128)S(1)}, s32[3]{0:T(128)}, u32[]{:S(2)}) %copy-start.4) | copy-done | bytes 36
  4.2 23.6 %shard_map.77 = (bf16[5,64,5248]{2,1,0:T(8,128)(2,1)S(1)}, f32[2,32,291]{2,1,0:T(8,128)S(1)}) custom-call(bf16[2,32,291]{2,1,0:T(8,128)(2,1)S(1)} %copy-done.1, bf16[80,291]{1,0:T(8,128)(2,1)S(1)} %bitcast.4, f32[80]{0:T(128)S(1)} %copy-done.2, s32[5]{0:T(128)S(1)} %copy-done.3, s32[3]{0:T(128)S(1)} %copy-done.4, bf16[5,64,5248]{2,1,0:T(8,128)(2,1)} %bitcast.5), custom_call_target="tpu_custom_call" | custom-call | tf_op jit(solution)/shard_map/pallas_call | solution.py:495
  27.8 1.7 %copy.10 = bf16[5,2,32,5248]{3,2,1,0:T(8,128)(2,1)} copy(bf16[5,2,32,5248]{3,2,1,0:T(8,128)(2,1)S(1)} %bitcast.3) | data formatting | bytes 6717440
  29.6 0.6 %copy.11 = f32[2,32,291]{2,1,0:T(8,128)} copy(f32[2,32,291]{2,1,0:T(8,128)S(1)} %get-tuple-element.9) | data formatting | bytes 148992
Async XLA Ops:
  0.6 0.8 %copy-start = (bf16[291,80]{0,1:T(8,128)(2,1)S(1)}, bf16[291,80]{0,1:T(8,128)(2,1)}, u32[]{:S(2)}) copy-start(bf16[291,80]{0,1:T(8,128)(2,1)} %param.8) | copy-start | bytes 139684
  1.5 0.8 %copy-start.1 = (bf16[2,32,291]{2,1,0:T(8,128)(2,1)S(1)}, bf16[2,32,291]{2,1,0:T(8,128)(2,1)}, u32[]{:S(2)}) copy-start(bf16[2,32,291]{2,1,0:T(8,128)(2,1)} %spec_hbm.1) | copy-start | bytes 111748
  2.3 0.7 %copy-start.2 = (f32[80]{0:T(128)S(1)}, f32[80]{0:T(128)}, u32[]{:S(2)}) copy-start(f32[80]{0:T(128)} %weights_hbm.1) | copy-start | bytes 964
  2.9 0.7 %copy-start.3 = (s32[5]{0:T(128)S(1)}, s32[5]{0:T(128)}, u32[]{:S(2)}) copy-start(s32[5]{0:T(128)} %cyc_hbm.1) | copy-start | bytes 64
  3.6 0.7 %copy-start.4 = (s32[3]{0:T(128)S(1)}, s32[3]{0:T(128)}, u32[]{:S(2)}) copy-start(s32[3]{0:T(128)} %pair_hbm.1) | copy-start | bytes 40

commit v3 on v2

--- a/solution.py
+++ b/solution.py
@@ -180,9 +180,9 @@
 
 def fused_kernel(
     n, slots, lats, levels, lat_count, points,
-    spec_hbm, leg_hbm, weights_hbm, cyc_hbm, pair_hbm, force_hbm,
+    table_ref, facts_ref, weights_ref, force_hbm,
     field_v, out_ref,
-    spec_ref, leg_ref, weights_ref, cyc_ref, pair_ref, small_sem, force_v, info, legm, coefm, send1, recv1, send2, recv2,
+    force_v, info, legm, coefm, send1, recv1, send2, recv2,
     pick, low, high_c, high_s, coef_z, back_z, twisted, prod,
     force_sem, info_ss, info_rs, f_ss, f_rs, b_ss, b_rs,
 ):
@@ -203,20 +203,11 @@
     def force_copy(q):
         return pltpu.make_async_copy(force_hbm.at[q], force_v.at[q], force_sem.at[q])
 
-    small = [
-        pltpu.make_async_copy(a, b, small_sem.at[i])
-        for i, (a, b) in enumerate(
-            (
-                (cyc_hbm, cyc_ref),
-                (pair_hbm, pair_ref),
-                (spec_hbm, spec_ref),
-                (leg_hbm, leg_ref),
-                (weights_hbm, weights_ref),
-            )
-        )
-    ]
-    for copy in small:
-        copy.start()
+    def cycle(q):
+        return facts_ref[0, LANES + q]
+
+    def pair(s):
+        return facts_ref[0, LANES + lats + s]
 
     barrier = pltpu.get_barrier_semaphore()
 
@@ -229,16 +220,14 @@
 
     for q in range(lats):
         force_copy(q).start()
-    small[0].wait()
-    small[1].wait()
 
     lane1 = lax.broadcasted_iota(i32, (1, LANES), 1)
     mine = jnp.full((1, LANES), -1.0, f32)
     for q in range(lats):
         for s in range(slots):
             k = q * slots + s
-            mine = jnp.where(lane1 == k, cyc_ref[q].astype(f32), mine)
-            mine = jnp.where(lane1 == GROUP + k, pair_ref[s].astype(f32), mine)
+            mine = jnp.where(lane1 == k, cycle(q), mine)
+            mine = jnp.where(lane1 == GROUP + k, pair(s), mine)
     info[me] = mine
 
     def remote(src, dst, ssem, rsem, to):
@@ -259,7 +248,7 @@
 
     @pl.loop(0, lats)
     def _(q):
-        length = jnp.full((1, LANES), NLON_EQ - 4 * cyc_ref[q], i32).astype(f32)
+        length = jnp.full((1, LANES), NLON_EQ - 4.0 * cycle(q), f32)
         inverse = 1.0 / length
         m_low = base + lax.broadcasted_iota(i32, (BLOCK, LANES), 1)
         v_low = lax.broadcasted_iota(i32, (BLOCK, LANES), 0)
@@ -273,22 +262,20 @@
         high_c[q] = c
         high_s[q] = s
 
-    for copy in small[2:]:
-        copy.wait()
-
-    lane = lax.broadcasted_iota(i32, (1, rows), 1)
+    lane = lax.broadcasted_iota(i32, (1, rows), 1).astype(f32)
     offset = lane
-    boundary = jnp.full((1, rows), 0, i32) + (window - pair_ref[0])
+    boundary = jnp.full((1, rows), window - pair(0), f32)
     for s in range(1, slots):
         here = lane >= s * row_count
         offset = jnp.where(here, lane - s * row_count, offset)
-        boundary = jnp.where(here, window - pair_ref[s], boundary)
+        boundary = jnp.where(here, window - pair(s), boundary)
     second = offset >= boundary
-    odd = (jnp.where(second, offset - boundary, offset) & 1) == 1
+    degree = jnp.where(second, offset - boundary, offset)
+    odd = degree - 2.0 * jnp.floor(0.5 * degree) > 0.5
     in_wave = [jnp.where(second, 0.0, 1.0), jnp.where(second, 1.0, 0.0)]
     sign = jnp.where(odd, -1.0, 1.0)
     for e in range(2):
-        values = spec_ref[e].astype(f32)
+        values = table_ref[e * levels : (e + 1) * levels].astype(f32)
         for w in range(2):
             north = values * in_wave[w]
             south = north * sign
@@ -313,7 +300,7 @@
     waves = column(GROUP)
     hot = jnp.where(cycles == lax.broadcasted_iota(i32, (total, LANES), 1), 1.0, 0.0)
     leg_all = lax.dot_general(
-        hot[:, :lat_count].astype(bf16), leg_ref[...], (((1,), (0,)), ((), ())),
+        hot[:, :lat_count].astype(bf16), table_ref[2 * levels : 2 * levels + lat_count], (((1,), (0,)), ((), ())),
         preferred_element_type=f32,
     )
 
@@ -371,7 +358,7 @@
         def _(q):
             if c == 0:
                 force_copy(q).wait()
-            length = NLON_EQ - 4 * cyc_ref[q]
+            length = NLON_EQ - 4.0 * cycle(q)
             acc_re = jnp.zeros((pairs, LANES), f32)
             acc_im = jnp.zeros((pairs, LANES), f32)
             for first in range(0, blocks, per):
@@ -402,7 +389,10 @@
                     ts = back[k * pairs : (k + 1) * pairs, LANES : 2 * LANES]
                     acc_re = acc_re + (tc * hc - ts * hs)
                     acc_im = acc_im - (tc * hs + ts * hc)
-            weight = weights_ref[cyc_ref[q]]
+            mine = lax.broadcasted_iota(i32, (1, LANES), 1).astype(f32) == cycle(q)
+            weight = jnp.sum(
+                jnp.where(mine, weights_ref[:, 0:LANES], 0.0), axis=1, keepdims=True
+            )
             for e, acc in ((0, acc_re), (1, acc_im)):
                 rounded = acc.astype(bf16).astype(f32)
                 north = rounded[0:part_levels]
@@ -468,7 +458,7 @@
     if u < whole:
         return f
     j = u * BLOCK + lax.broadcasted_iota(jnp.int32, f.shape, 1)
-    return jnp.where(j < length, f, 0.0)
+    return jnp.where(j.astype(jnp.float32) < length, f, 0.0)
 
 
 def on_device(n, spec_in, forcing, legendre, weights, cycle_slots, wave_pairs):
@@ -492,21 +482,20 @@
     low_shape = (lats, BLOCK, 2 * LANES)
     high_shape = (lats, high_rows, LANES)
     message = pltpu.VMEM((chunks, n, GROUP, 2 * half), bf16)
+    whole = jnp.pad(cycle_slots, (LANES, LANES - lats)) + jnp.pad(
+        wave_pairs, (LANES + lats, LANES - lats - slots)
+    )
+    facts = whole.astype(f32) + jnp.pad(weights, (0, 2 * LANES - lat_count))
+    facts = facts.reshape(1, 2 * LANES)
     field, spec_out = pl.pallas_call(
         functools.partial(fused_kernel, n, slots, lats, levels, lat_count, points),
         out_shape=(
             jax.ShapeDtypeStruct((lats, 2 * levels, points), bf16),
             jax.ShapeDtypeStruct((2, levels, rows), f32),
         ),
-        in_specs=[hbm] * 6,
+        in_specs=[vmem, pl.BlockSpec(memory_space=pltpu.SMEM), vmem, hbm],
         out_specs=(vmem, vmem),
         scratch_shapes=[
-            pltpu.VMEM((2, levels, rows), bf16),
-            pltpu.VMEM((lat_count, rows), bf16),
-            pltpu.SMEM((lat_count,), f32),
-            pltpu.SMEM((lats,), jnp.int32),
-            pltpu.SMEM((slots,), jnp.int32),
-            dma((5,)),
             pltpu.VMEM((lats, 2 * levels, points), bf16),
             pltpu.VMEM((n, 1, LANES), f32),
             pltpu.VMEM((total, rows), bf16),
@@ -528,7 +517,7 @@
             vmem_limit_bytes=49 * 1024 * 1024 + 512 * 1024,
         ),
     )(
-        spec_in, legendre.T, weights, cycle_slots, wave_pairs,
+        jnp.concatenate([spec_in.reshape(2 * levels, rows), legendre.T]), facts, facts,
         forcing.reshape(lats, 2 * levels, points),
     )
     return field.reshape(lats, 2, levels, points), spec_out

time: 30.5 us -> 28.8 us (0.944)
  local copies, waits for them, and re-layouts: 5.96 us -> 2.38 us
  other arithmetic: 0 us -> 1.61 us
  Pallas kernels: 23.6 us -> 24 us
    unnamed x12 -> x2, local copies, waits for them, and re-layouts: 5.96 us -> 2.38 us
    concatenate x0 -> x1, other arithmetic: none -> 0.84 us  [on_device(): jnp.concatenate([spec_in.reshape(2 * levels, rows), legendre.T])]
    add x0 -> x1, other arithmetic: none -> 0.77 us  [on_device(): facts = whole.astype(f32) + jnp.pad(weights, (0, 2 * LANES - lat_count))]
    pallas_call x1, Pallas kernels: 23.6 us -> 24 us  [on_device(): pl.pallas_call(functools.partial(fused_kernel, n, slots, lats, levels, la...]
where the time goes in v3:
time: 28.8 us; the launch traced here: 28.6 us
  Pallas kernels  24 us (83%)
  local copies, waits for them, and re-layouts  2.38 us (8%)
  other arithmetic  1.61 us (6%)
  between operations  0.64 us (2%)
    pallas_call x1, Pallas kernels, on_device(): pl.pallas_call(functools.partial(fused_kernel, n, slots, lats, levels, la...  24 us
    unnamed x2, local copies, waits for them, and re-layouts  2.38 us
    concatenate x1, other arithmetic, on_device(): jnp.concatenate([spec_in.reshape(2 * levels, rows), legendre.T])  0.84 us
    add x1, other arithmetic, on_device(): facts = whole.astype(f32) + jnp.pad(weights, (0, 2 * LANES - lat_count))  0.77 us

profile of v3, /device:TPU:0, one launch (start us, length us, event | category | flops | bytes accessed | tf_op | source)
XLA Modules:
  0.0 28.6 jit_solution(804875339210692903)
XLA Ops:
  0.6 0.8 %pad_add_fusion = f32[256]{0:T(256)S(1)} fusion(f32[80]{0:T(128)} %param.9, s32[3]{0:T(128)} %param.11, s32[5]{0:T(128)} %param.10), kind=kLoop, calls=%fused_computation.1 | loop fusion | flops 768 | bytes 1376 | tf_op jit(solution)/shard_map/add | solution.py:488
  1.4 0.8 %pad_maximum_fusion.table_ref = bf16[144,291]{1,0:T(8,128)(2,1)S(1)} fusion(bf16[80,291]{1,0:T(8,128)(2,1)} %bitcast.9, bf16[64,291]{1,0:T(8,128)(2,1)} %bitcast.10), kind=kLoop, calls=%fused_computation | loop fusion | flops 167616 | bytes 167616 | tf_op jit(solution)/shard_map/concatenate | solution.py:520
  2.2 24.0 %shard_map.77 = (bf16[5,64,5248]{2,1,0:T(8,128)(2,1)S(1)}, f32[2,32,291]{2,1,0:T(8,128)S(1)}) custom-call(bf16[144,291]{1,0:T(8,128)(2,1)S(1)} %pad_maximum_fusion.table_ref, f32[1,256]{1,0:T(1,128)S(1)} %bitcast.6, f32[1,256]{1,0:T(1,128)S(1)} %bitcast.7, bf16[5,64,5248]{2,1,0:T(8,128)(2,1)} %bitcast.8), custom_call_target="tpu_custom_call" | custom-call | tf_op jit(solution)/shard_map/pallas_call | solution.py:490
  26.2 1.7 %copy.10 = bf16[5,2,32,5248]{3,2,1,0:T(8,128)(2,1)} copy(bf16[5,2,32,5248]{3,2,1,0:T(8,128)(2,1)S(1)} %bitcast.5) | data formatting | bytes 6717440
  28.0 0.6 %copy.11 = f32[2,32,291]{2,1,0:T(8,128)} copy(f32[2,32,291]{2,1,0:T(8,128)S(1)} %get-tuple-element.9) | data formatting | bytes 148992

commit v4 on v3

--- a/solution.py
+++ b/solution.py
@@ -214,7 +214,7 @@
     def peer(i):
         return lax.rem(me + i, n)
 
-    @pl.loop(1, n)
+    @pl.loop(1, n, unroll=n - 1)
     def _(i):
         pl.semaphore_signal(barrier, inc=1, device_id=(part, peer(i)), device_id_type=MESH)
 
@@ -242,7 +242,7 @@
 
     pl.semaphore_wait(barrier, n - 1)
 
-    @pl.loop(1, n)
+    @pl.loop(1, n, unroll=n - 1)
     def _(i):
         remote(info.at[me], info.at[me], info_ss.at[0], info_rs.at[0], peer(i)).start()
 
@@ -323,7 +323,7 @@
 
     for c in range(chunks):
 
-        @pl.loop(1, n)
+        @pl.loop(1, n, unroll=n - 1)
         def _(i):
             to = peer(i)
             remote(send1.at[c, to], recv1.at[c, me], f_ss.at[c], f_rs.at[c], to).start()
@@ -409,7 +409,7 @@
         )
         send2[c] = z.astype(bf16).reshape(n, GROUP, 2 * half)
 
-        @pl.loop(1, n)
+        @pl.loop(1, n, unroll=n - 1)
         def _(i):
             to = peer(i)
             remote(send2.at[c, to], recv2.at[c, me], b_ss.at[c], b_rs.at[c], to).start()

time: 28.8 us -> 28.7 us (level)
  no operation moved by 1% of the time
where the time goes in v4:
time: 28.7 us; the launch traced here: 28.6 us
  Pallas kernels  23.9 us (83%)
  local copies, waits for them, and re-layouts  2.38 us (8%)
  other arithmetic  1.61 us (6%)
  between operations  0.64 us (2%)
    pallas_call x1, Pallas kernels, on_device(): pl.pallas_call(functools.partial(fused_kernel, n, slots, lats, levels, la...  23.9 us
    unnamed x2, local copies, waits for them, and re-layouts  2.38 us
    concatenate x1, other arithmetic, on_device(): jnp.concatenate([spec_in.reshape(2 * levels, rows), legendre.T])  0.84 us
    add x1, other arithmetic, on_device(): facts = whole.astype(f32) + jnp.pad(weights, (0, 2 * LANES - lat_count))  0.77 us

profile of v4, /device:TPU:0, one launch (start us, length us, event | category | flops | bytes accessed | tf_op | source)
XLA Modules:
  0.0 28.6 jit_solution(8884802546384384833)
XLA Ops:
  0.6 0.8 %pad_add_fusion = f32[256]{0:T(256)S(1)} fusion(f32[80]{0:T(128)} %param.9, s32[3]{0:T(128)} %param.11, s32[5]{0:T(128)} %param.10), kind=kLoop, calls=%fused_computation.1 | loop fusion | flops 768 | bytes 1376 | tf_op jit(solution)/shard_map/add | solution.py:488
  1.4 0.8 %pad_maximum_fusion.table_ref = bf16[144,291]{1,0:T(8,128)(2,1)S(1)} fusion(bf16[80,291]{1,0:T(8,128)(2,1)} %bitcast.9, bf16[64,291]{1,0:T(8,128)(2,1)} %bitcast.10), kind=kLoop, calls=%fused_computation | loop fusion | flops 167616 | bytes 167616 | tf_op jit(solution)/shard_map/concatenate | solution.py:520
  2.2 23.9 %shard_map.77 = (bf16[5,64,5248]{2,1,0:T(8,128)(2,1)S(1)}, f32[2,32,291]{2,1,0:T(8,128)S(1)}) custom-call(bf16[144,291]{1,0:T(8,128)(2,1)S(1)} %pad_maximum_fusion.table_ref, f32[1,256]{1,0:T(1,128)S(1)} %bitcast.6, f32[1,256]{1,0:T(1,128)S(1)} %bitcast.7, bf16[5,64,5248]{2,1,0:T(8,128)(2,1)} %bitcast.8), custom_call_target="tpu_custom_call" | custom-call | tf_op jit(solution)/shard_map/pallas_call | solution.py:490
  26.2 1.7 %copy.10 = bf16[5,2,32,5248]{3,2,1,0:T(8,128)(2,1)} copy(bf16[5,2,32,5248]{3,2,1,0:T(8,128)(2,1)S(1)} %bitcast.5) | data formatting | bytes 6717440
  27.9 0.6 %copy.11 = f32[2,32,291]{2,1,0:T(8,128)} copy(f32[2,32,291]{2,1,0:T(8,128)S(1)} %get-tuple-element.9) | data formatting | bytes 148992
